TPU v7x, 128 devices: a whole 4x4x4 slice. The times are simulated.
128 devices in a mesh: member: 8 (over x, z_hi), space: 16 (over y, z_lo, core).
Axes of the slice: x: 4, y: 4, z: 4 (z_hi: 2, z_lo: 2; z = z_hi * 2 + z_lo), core: 2. Of those that a mesh axis runs over, the one named last changes fastest.
Arguments:
- fields: bfloat16 [8, 100, 65536], P('member', None, 'space'), may hold values from -6 to 6
- target: bfloat16 [100, 65536], P(None, 'space'), may hold values from -6 to 6
- area_weights: float32 [65536], P('space'), may hold values from 0.25 to 5.25, as said below
- hidden: bfloat16 [8, 65536, 1024], P('member', 'space'), may hold values from -6 to 6
- w_in: bfloat16 [1024, 1024], replicated, may hold values from -0.1875 to 0.1875
- w_out: bfloat16 [100, 1024], replicated, may hold values from -0.75 to 0.75
Outputs:
- loss: float32 [], replicated
- grad_hidden: bfloat16 [8, 65536, 1024], P('member', 'space')
- grad_w1: float32 [1024, 1024], P(('member', 'space'))
Inputs may be any that keep to these rules, and one draw needn't show every extreme that they name: `area_weights`: positive area weights.
All inputs are finite; a program needn't handle non-finite values.
Results may differ from a plain program's by a relative error of at most 0.0057.
Values may be sent and summed in bfloat16 or wider, within the bound.
A program may use at most 128 MiB of HBM per device.

v0:
```python
import math

import jax
import jax.numpy as jnp
from jax import lax
from jax.sharding import PartitionSpec as P

alpha_fair = 0.95


def gelu_back(pre, upstream):
    return jax.vjp(jax.nn.gelu, pre)[1](upstream)[0]


def on_device(fields, target, area_weights, hidden, w_in, w_out):
    count = lax.axis_size("member")
    spaces = lax.axis_size("space")
    fair = (1.0 - alpha_fair) / count
    coef = (1.0 - fair) / (count * (count - 1))
    own = fields[0].astype(jnp.float32)
    truth = target.astype(jnp.float32)
    weights = area_weights[None, :]
    gap = own[None] - lax.all_gather(fields, "member", axis=0, tiled=True).astype(jnp.float32)
    spread = jnp.sum(jnp.abs(gap), 0)
    signs = jnp.sum(jnp.sign(gap), 0)
    pull = coef * weights * signs
    npoints = fields.shape[2] * spaces
    local_loss = jnp.sum(weights * (jnp.abs(own - truth) / count - 0.5 * coef * spread))
    loss = lax.psum(local_loss, ("member", "space")) / (fields.shape[1] * npoints)
    slope = (weights * jnp.sign(own - truth) / count - pull).astype(jnp.bfloat16)
    feats = hidden[0]
    pre = jnp.dot(feats, w_in, preferred_element_type=jnp.float32)
    upstream = lax.dot_general(
        slope, w_out, (((0,), (0,)), ((), ())), preferred_element_type=jnp.float32
    )
    delta = gelu_back(pre, upstream).astype(jnp.bfloat16)
    grad_feats = lax.dot_general(
        delta, w_in, (((1,), (1,)), ((), ())), preferred_element_type=jnp.float32
    ).astype(jnp.bfloat16)
    summed = lax.psum_scatter(
        lax.dot_general(feats, delta, (((0,), (0,)), ((), ())), preferred_element_type=jnp.float32),
        ("member", "space"),
        scatter_dimension=0,
        tiled=True,
    )
    grad_w1 = summed * (1.0 / math.sqrt(npoints))
    return (loss, grad_feats[None], grad_w1)


def solution(mesh):
    return jax.shard_map(
        on_device,
        mesh=mesh,
        in_specs=(
            P("member", None, "space"),
            P(None, "space"),
            P("space"),
            P("member", "space", None),
            P(),
            P(),
        ),
        out_specs=(P(), P("member", "space", None), P(("member", "space"), None)),
        check_vma=False,
    )
```

profile of v0, /device:TPU:0, one launch (start us, length us, event | category | flops | bytes accessed | tf_op | source)
XLA Modules:
  0.0 804.7 jit_solution(5526988450193909224)
XLA Ops:
  7.2 0.0 copy-start
  7.2 0.0 all-gather.2.cloned.1.call-start
  7.2 0.7 all-gather.2.cloned.1.call-update
  7.9 0.0 reduce-scatter.4.cloned.1.call-start
  8.0 0.7 broadcast_multiply_fusion.1
  8.7 2.5 bitcast_convert_fusion
  11.2 0.0 copy-done
  11.2 14.6 %fusion.9 = f32[4096,1024]{1,0:T(8,128)} fusion(bf16[1024,1024]{1,0:T(8,128)(2,1)S(1)} %copy-done, bf16[1,4096,1024]{2,1,0:T(8,128)(2,1)} %param.9), kind=kOutput, calls=%fused_computation.14 | convolution fusion | flops 8589934592 | bytes 27262976 | tf_op jit(solution)/shard_map/dot_general | solution.py:32
  25.8 0.0 copy-start.1
  25.8 0.0 copy-start.3
  25.8 0.0 copy-start.4
  25.8 81.5 %all-gather.2.cloned.1.call-done = bf16[8,100,4096]{2,1,0:T(8,128)(2,1)} async-done(((bf16[1,100,4096]{2,1,0:T(8,128)(2,1)}), bf16[8,100,4096]{2,1,0:T(8,128)(2,1)}) %all-gather.2.cloned.1.call-update) | async-done | bytes 6553616 | tf_op jit(solution)/shard_map/all_gather | solution.py:23
  107.3 0.0 copy-start.2
  107.3 0.0 slice-start
  107.3 10.6 %sign_reduce_fusion = (f32[100,4096]{1,0:T(8,128)S(1)}, f32[100,4096]{1,0:T(8,128)}) fusion(bf16[8,100,4096]{2,1,0:T(8,128)(2,1)} %all-gather.2.cloned.1.call-done, f32[100,4096]{1,0:T(8,128)} %bitcast_convert_fusion), kind=kLoop, calls=%fused_computation.9 | loop fusion | flops 18841600 | bytes 11468800 | tf_op jit(solution)/shard_map/reduce_sum | solution.py:25
  117.9 0.0 copy-done.1
  117.9 0.0 copy-done.3
  117.9 0.0 copy-done.4
  117.9 0.0 copy-done.2
  117.9 0.0 slice-start.1
  117.9 16.5 %fusion.6 = bf16[4096,1024]{1,0:T(8,128)(2,1)} fusion(f32[4096,1024]{1,0:T(8,128)} %fusion.9, bf16[100,1024]{1,0:T(8,128)(2,1)S(1)} %copy-done.4, f32[100,4096]{1,0:T(8,128)S(1)} %get-tuple-element.9, bf16[100,4096]{1,0:T(8,128)(2,1)S(1)} %copy-done.2, bf16[1,100,4096]{2,1,0:T(8,128)(2,1)S(1)} %copy-done.1, f32[4096]{0:T(1024)S(1)} %broadcast_multiply_fusion.1, ...), kind=kOutput, calls=%fused_computation.8 | convolution fusion | flops 926433280 | bytes 28680192 | tf_op jit(solution)/shard_map/dot_general | solution.py:33
  134.4 0.0 slice-done
  134.4 0.0 slice-done.1
  134.4 12.6 %fusion.11 = f32[1024,1024]{0,1:T(8,128)} fusion(bf16[4096,1024]{1,0:T(8,128)(2,1)} %fusion.6, bf16[1,4096,1024]{2,1,0:T(8,128)(2,1)S(1)} %bitcast.26), kind=kOutput, calls=%fused_computation.17 | convolution fusion | flops 8589934592 | bytes 20971520 | tf_op jit(solution)/shard_map/dot_general | solution.py:41
  147.1 5.3 copy.11
  152.4 0.0 reduce-scatter.4.cloned.1.call-update
  152.4 2.8 multiply_reduce_fusion
  155.2 65.0 %psum.7 = f32[]{:T(128)} all-reduce(f32[]{:T(128)} %multiply_reduce_fusion), channel_id=1, replica_groups=mesh['member'=8,'space'=16] {'member','space'}, use_global_device_ids=true, to_apply=%region_2.0 | all-reduce | flops 1 | bytes 8 | tf_op jit(solution)/shard_map/psum | solution.py:29
  220.9 14.6 %convert_bitcast_fusion = bf16[1,4096,1024]{2,1,0:T(8,128)(2,1)} fusion(bf16[4096,1024]{1,0:T(8,128)(2,1)} %fusion.6, bf16[1024,1024]{1,0:T(8,128)(2,1)S(1)} %copy-done), kind=kOutput, calls=%fused_computation.16 | convolution fusion | flops 8594128896 | bytes 18874368 | tf_op jit(solution)/shard_map/dot_general | solution.py:37
  235.5 559.5 %reduce-scatter.4.cloned.1.call-done = f32[8,1024]{1,0:T(8,128)} async-done(((f32[1024,1024]{1,0:T(8,128)}), f32[8,1024]{1,0:T(8,128)}) %reduce-scatter.4.cloned.1.call-update) | async-done | bytes 32784
  794.9 0.9 copy.12
  795.9 0.8 copy.10
  (2 shorter events, 0.0 us)
Async XLA Ops:
  7.2 4.0 copy-start
  7.2 100.1 %all-gather.2.cloned.1.call-start = ((), (), s32[]{:S(2)}) async-start(), calls=%async_computation.1 | async-start | bytes 7667712 | tf_op jit(solution)/shard_map/all_gather | solution.py:23
  7.9 787.0 %reduce-scatter.4.cloned.1.call-start = ((), (), s32[]{:S(2)}) async-start(), calls=%async_computation.2 | async-start | bytes 4227072
  25.8 92.1 %copy-start.1 = (bf16[1,100,4096]{2,1,0:T(8,128)(2,1)S(1)}, bf16[1,100,4096]{2,1,0:T(8,128)(2,1)}, u32[]{:S(2)}) copy-start(bf16[1,100,4096]{2,1,0:T(8,128)(2,1)} %param.6) | copy-start | bytes 2457604
  25.8 92.1 %copy-start.3 = (f32[4096]{0:T(1024)S(1)}, f32[4096]{0:T(1024)}, u32[]{:S(2)}) copy-start(f32[4096]{0:T(1024)} %param.8) | copy-start | bytes 49156
  25.8 92.1 %copy-start.4 = (bf16[100,1024]{1,0:T(8,128)(2,1)S(1)}, bf16[100,1024]{1,0:T(8,128)(2,1)}, u32[]{:S(2)}) copy-start(bf16[100,1024]{1,0:T(8,128)(2,1)} %param.11) | copy-start | bytes 614404
  107.3 10.6 %copy-start.2 = (bf16[100,4096]{1,0:T(8,128)(2,1)S(1)}, bf16[100,4096]{1,0:T(8,128)(2,1)}, u32[]{:S(2)}) copy-start(bf16[100,4096]{1,0:T(8,128)(2,1)} %param.7) | copy-start | bytes 2457604
  107.3 27.1 %slice-start = ((s8[8388608]{0:T(1024)(128)(4,1)}), s8[4194304]{0:T(1024)(128)(4,1)S(1)}, s32[]{:S(2)}) async-start(s8[8388608]{0:T(1024)(128)(4,1)} %bitcast.25), calls=%async_computation.3 | async-start | bytes 8388608
  117.9 16.5 %slice-start.1 = ((s8[8388608]{0:T(1024)(128)(4,1)}), s8[4194304]{0:T(1024)(128)(4,1)S(1)}, s32[]{:S(2)}) async-start(s8[8388608]{0:T(1024)(128)(4,1)} %bitcast.25), calls=%async_computation.4 | async-start | bytes 8388608
Sparse Core Ops, SparseCore 0:
  10.3 96.9 all-gather.1
  152.6 642.3 reduce-scatter.3
where the time goes:
time: 805 us
  waiting for transfers between devices  642 us (80%)
  blocking collectives  65 us (8%)
  matrix products  58.3 us (7%)
  other arithmetic  16.6 us (2%)
  between operations  15.9 us (2%)
    unnamed x3, waiting for transfers between devices  560 us
    all_gather x1, waiting for transfers between devices, on_device(): lax.all_gather(fields, 'member', axis=0, tiled=True).astype(jnp.float32)  81.5 us
    psum x1, blocking collectives, on_device(): lax.psum(local_loss, ('member', 'space')) / (fields.shape[1] * npoints)  65 us
    dot_general x1, matrix products, on_device(): lax.dot_general(slope, w_out, (((0,), (0,)), ((), ())), preferred_element...  16.5 us
  transfers between devices with their start and end apart: 2, of which 2 were waited for; matrix products, arithmetic and copies ran while one was open for 4% of the time, Pallas kernels for 0%

commit v1 on v0

v1 whole, which is shorter than its diff:
```python
import functools
import math

import jax
import jax.numpy as jnp
from jax import lax
from jax.experimental import pallas as pl
from jax.experimental.pallas import tpu as pltpu
from jax.sharding import PartitionSpec as P

ALPHA_FAIR = 0.95
MEMBERS, SPACES = 8, 16
CHANNELS, LOCAL, HID = 100, 4096, 1024
PART = LOCAL // MEMBERS
ROOT = math.sqrt(2.0 / math.pi)
CUBIC = 0.044715
F32, BF16 = jnp.float32, jnp.bfloat16
MESH = pl.DeviceIdType.MESH

ORDERS = ((0, 1, 2), (1, 2, 0), (2, 0, 1), (0, 2, 1))
BLOCKS = len(ORDERS)


def gelu_slope(u):
    s = u * u
    t = jnp.tanh(u * (ROOT + (ROOT * CUBIC) * s))
    return 0.5 * (1.0 + t) + (1.0 - t * t) * (u * (0.5 * ROOT + (1.5 * ROOT * CUBIC) * s))


def sign(d):
    return jnp.where(d > 0.0, 1.0, jnp.where(d < 0.0, -1.0, 0.0))


class Place:
    def __init__(self):
        self.member = lax.axis_index("member")
        self.space = lax.axis_index("space")
        x, z_hi = self.member // 2, self.member % 2
        y, z_lo = self.space // 4, (self.space // 2) % 2
        self.core = self.space % 2
        self.at = (x, y, z_hi * 2 + z_lo)

    def far(self, axis, d):
        return (self.at[axis] + d) % 4

    def device(self, at, core):
        x, y, z = at
        return {"member": x * 2 + z // 2, "space": (y * 2 + z % 2) * 2 + core}

    def along(self, axis, d):
        at = list(self.at)
        at[axis] = self.far(axis, d)
        return self.device(at, self.core)

    def other_core(self):
        return self.device(self.at, 1 - self.core)

    def other_member(self, d):
        return {"member": (self.member + d) % MEMBERS, "space": self.space}


def forward_kernel(
    fields, target, area, hidden, w_in, w_out,
    loss_out, du_out, grad_out,
    hid, win, wout, slope, du,
    got, truth, weight, back, dx,
    sums, half0, sum1, part1, sum2, part2, sum3, part3,
    lacc, lsum, lpart,
    local_sem, hid_sem, out_sem, field_sems, back_sems, rs_sems, loss_sems,
):
    here = Place()
    me = here.member
    count = MEMBERS
    fair = (1.0 - ALPHA_FAIR) / count
    coef = (1.0 - fair) / (count * (count - 1))

    mine = pl.ds(pl.multiple_of(me * PART, PART), PART)
    locals_ = [
        pltpu.make_async_copy(src, dst, local_sem.at[i])
        for i, (src, dst) in enumerate((
            (fields.at[0, :, mine], got.at[me]),
            (target.at[:, mine], truth),
            (area.at[:, mine], weight),
            (w_in, win),
            (w_out, wout),
        ))
    ]
    for copy in locals_:
        copy.start()

    def rows_of(c):
        return pl.ds(c * PART, PART)

    loads = [
        pltpu.make_async_copy(hidden.at[0, rows_of(c)], hid.at[rows_of(c)], hid_sem.at[c])
        for c in range(MEMBERS)
    ]
    for copy in loads:
        copy.start()

    barrier = pltpu.get_barrier_semaphore()
    others = [here.other_member(d) for d in range(1, MEMBERS)]
    others += [here.other_core()]
    others += [here.along(1, d) for d in range(1, 4)]
    others += [here.along(2, d) for d in (1, 3)]
    for device in others:
        pl.semaphore_signal(barrier, inc=1, device_id=device, device_id_type=MESH)
    pl.semaphore_wait(barrier, len(others))

    def field_copy(d):
        to = (me + d) % MEMBERS
        return pltpu.make_async_remote_copy(
            src_ref=fields.at[0, :, pl.ds(pl.multiple_of(to * PART, PART), PART)],
            dst_ref=got.at[me],
            send_sem=field_sems.at[0, d - 1],
            recv_sem=field_sems.at[1, d - 1],
            device_id=here.other_member(d),
            device_id_type=MESH,
        )

    def field_arrival(d):
        slot = got.at[(me + MEMBERS - d) % MEMBERS]
        return pltpu.make_async_remote_copy(
            src_ref=slot, dst_ref=slot,
            send_sem=field_sems.at[0, d - 1], recv_sem=field_sems.at[1, d - 1],
            device_id=here.other_member(MEMBERS - d), device_id_type=MESH,
        )

    field_copies = [field_copy(d) for d in range(1, MEMBERS)]
    for copy in field_copies:
        copy.start()

    def project(c):
        loads[c].wait()
        u = jnp.dot(hid[rows_of(c), :], win[...], preferred_element_type=F32)
        slope[rows_of(c), :] = gelu_slope(u)

    locals_[3].wait()
    for c in range(4):
        project(c)

    for copy in locals_[:3]:
        copy.wait()
    for d in range(1, MEMBERS):
        field_arrival(d).wait_recv()
    lacc[...] = jnp.zeros_like(lacc)

    def compare(start, rows):
        at = pl.ds(start, rows)
        for j in range(0, PART, 128):
            lanes = pl.ds(j, 128)
            x = [got[k, at, lanes].astype(F32) for k in range(MEMBERS)]
            y = truth[at, lanes].astype(F32)
            w = weight[:, lanes]
            pull = coef * w
            signs = [0.0] * MEMBERS
            spread = 0.0
            for a in range(MEMBERS):
                for b in range(a + 1, MEMBERS):
                    d = x[a] - x[b]
                    s = sign(d)
                    spread = spread + jnp.abs(d)
                    signs[a] = signs[a] + s
                    signs[b] = signs[b] - s
            miss = 0.0
            for k in range(MEMBERS):
                e = x[k] - y
                miss = miss + jnp.abs(e)
                back[k, at, lanes] = (w * sign(e) / count - pull * signs[k]).astype(BF16)
            lacc[pl.ds(0, rows), :] += w * (miss / count - coef * spread)

    def compare_rows(i, _):
        compare(pl.multiple_of(i * 16, 16), 16)
        return 0

    whole = CHANNELS // 16
    lax.fori_loop(0, whole, compare_rows, 0)
    compare(whole * 16, CHANNELS - whole * 16)

    def back_copy(d):
        to = (me + d) % MEMBERS
        return pltpu.make_async_remote_copy(
            src_ref=back.at[to],
            dst_ref=dx.at[me],
            send_sem=back_sems.at[0, d - 1],
            recv_sem=back_sems.at[1, d - 1],
            device_id=here.other_member(d),
            device_id_type=MESH,
        )

    def back_arrival(d):
        slot = dx.at[(me + MEMBERS - d) % MEMBERS]
        return pltpu.make_async_remote_copy(
            src_ref=slot, dst_ref=slot,
            send_sem=back_sems.at[0, d - 1], recv_sem=back_sems.at[1, d - 1],
            device_id=here.other_member(MEMBERS - d), device_id_type=MESH,
        )

    back_copies = [back_copy(d) for d in range(1, MEMBERS)]
    for copy in back_copies:
        copy.start()
    own_back = pltpu.make_async_copy(back.at[me], dx.at[me], local_sem.at[0])
    own_back.start()

    loss_copies = []

    def loss_send(stage):
        copies = []
        for d in (1,) if stage == 0 else (1, 2, 3):
            k = d - 1 if stage == 0 else 1 + (stage - 1) * 3 + d - 1
            copies.append(pltpu.make_async_remote_copy(
                src_ref=lsum.at[stage],
                dst_ref=lpart.at[k],
                send_sem=loss_sems.at[0, k],
                recv_sem=loss_sems.at[1, k],
                device_id=here.other_core() if stage == 0 else here.along(stage - 1, d),
                device_id_type=MESH,
            ))
        for copy in copies:
            copy.start()
        loss_copies.append(copies)

    def loss_sum(stage):
        total = lsum[stage]
        first = 0 if stage == 0 else 1 + (stage - 1) * 3
        for d, copy in enumerate(loss_copies[stage]):
            copy.wait_recv()
            total = total + lpart[first + d]
        lsum[stage + 1] = total

    lsum[0] = lacc[0:8, :] + lacc[8:16, :]
    loss_send(0)
    for c in range(4, MEMBERS):
        project(c)
        loss_sum(c - 4)
        if c < 7:
            loss_send(c - 3)
    loss_out[0, 0] = jnp.sum(lsum[4]) / (CHANNELS * LOCAL * SPACES)

    locals_[4].wait()
    own_back.wait()
    for d in range(1, MEMBERS):
        back_arrival(d).wait_recv()
    stores = []
    for c in range(MEMBERS):
        dv = lax.dot_general(
            dx[c], wout[...], (((0,), (0,)), ((), ())), preferred_element_type=F32
        )
        du[rows_of(c), :] = (dv * slope[rows_of(c), :]).astype(BF16)
        copy = pltpu.make_async_copy(du.at[rows_of(c)], du_out.at[rows_of(c)], out_sem.at[c])
        copy.start()
        stores.append(copy)

    def weight_grad(h, i):
        g = lax.dot_general(
            hid[:, pl.ds(i * 512, 512)], du[:, pl.ds(h * 512, 512)],
            (((0,), (0,)), ((), ())), preferred_element_type=F32,
        )
        for r in range(64):
            at = (2 * i + r // 32, (r // 4) % 4, ((r // 16) % 2) * 2 + (r // 2) % 2)
            rows = g[8 * r : 8 * r + 8]
            for q in range(2):
                b = 2 * h + q
                p = [at[axis] for axis in ORDERS[b]]
                pair = jnp.concatenate(
                    [rows[:, 256 * q : 256 * q + 128], rows[:, 256 * q + 128 : 256 * q + 256]], 0
                )
                sums[b, r % 2, p[0], p[1], p[2]] = pair.astype(BF16)

    rs_copies = {}

    def rs_send(b, stage):
        copies = []
        if stage == 0:
            copies.append(pltpu.make_async_remote_copy(
                src_ref=sums.at[b, 1 - here.core], dst_ref=half0.at[b],
                send_sem=rs_sems.at[0, b, 0], recv_sem=rs_sems.at[1, b, 0],
                device_id=here.other_core(), device_id_type=MESH,
            ))
        else:
            axis = ORDERS[b][stage - 1]
            src, dst = ((sum1, part1), (sum2, part2), (sum3, part3))[stage - 1]
            for d in (2, 1, 3):
                k = 1 + (stage - 1) * 3 + d - 1
                copies.append(pltpu.make_async_remote_copy(
                    src_ref=src.at[b, here.far(axis, d)], dst_ref=dst.at[b, d - 1],
                    send_sem=rs_sems.at[0, b, k], recv_sem=rs_sems.at[1, b, k],
                    device_id=here.along(axis, d), device_id_type=MESH,
                ))
        for copy in copies:
            copy.start()
        rs_copies[b, stage] = copies

    def rs_sum(b, stage):
        for copy in rs_copies[b, stage]:
            copy.wait_recv()
        if stage == 0:
            for p in range(4):
                sum1[b, p] = (
                    sums[b, here.core, p].astype(F32) + half0[b, p].astype(F32)
                ).astype(BF16)
            return
        src, dst = ((sum1, part1), (sum2, part2), (sum3, part3))[stage - 1]
        total = src[b, here.at[ORDERS[b][stage - 1]]].astype(F32)
        for d in range(3):
            total = total + dst[b, d].astype(F32)
        if stage == 3:
            total = total * (1.0 / math.sqrt(LOCAL * SPACES))
            grad_out[:, pl.ds(256 * b, 128)] = total[0:8]
            grad_out[:, pl.ds(256 * b + 128, 128)] = total[8:16]
        else:
            (sum2, sum3)[stage - 1][b] = total.astype(BF16)

    def step(blocks, stage):
        for b in blocks:
            rs_sum(b, stage)
            if stage < 3:
                rs_send(b, stage + 1)

    early, late = (0, 1), (2, 3)
    weight_grad(0, 0)
    weight_grad(0, 1)
    for b in early:
        rs_send(b, 0)
    weight_grad(1, 0)
    step(early, 0)
    weight_grad(1, 1)
    for b in late:
        rs_send(b, 0)
    step(early, 1)
    step(late, 0)
    step(early, 2)
    step(late, 1)
    step(early, 3)
    step(late, 2)
    step(late, 3)

    for copy in stores:
        copy.wait()
    for copy in field_copies + back_copies:
        copy.wait_send()
    for copies in loss_copies + list(rs_copies.values()):
        for copy in copies:
            copy.wait_send()


def backward_kernel(du, w_in, out):
    out[0] = lax.dot_general(
        du[...], w_in[...], (((1,), (1,)), ((), ())), preferred_element_type=F32
    ).astype(BF16)


def on_device(fields, target, area_weights, hidden, w_in, w_out):
    anywhere = pl.BlockSpec(memory_space=pl.ANY)
    vmem = pl.BlockSpec(memory_space=pltpu.VMEM)
    dma = pltpu.SemaphoreType.DMA
    tile = (16, 128)
    loss, du, grad_w1 = pl.pallas_call(
        forward_kernel,
        out_shape=(
            jax.ShapeDtypeStruct((1, 1), F32),
            jax.ShapeDtypeStruct((LOCAL, HID), BF16),
            jax.ShapeDtypeStruct((8, HID), F32),
        ),
        in_specs=[anywhere] * 6,
        out_specs=(pl.BlockSpec(memory_space=pltpu.SMEM), anywhere, vmem),
        scratch_shapes=[
            pltpu.VMEM((LOCAL, HID), BF16),
            pltpu.VMEM((HID, HID), BF16),
            pltpu.VMEM((CHANNELS, HID), BF16),
            pltpu.VMEM((LOCAL, HID), F32),
            pltpu.VMEM((LOCAL, HID), BF16),
            pltpu.VMEM((MEMBERS, CHANNELS, PART), BF16),
            pltpu.VMEM((CHANNELS, PART), BF16),
            pltpu.VMEM((1, PART), F32),
            pltpu.VMEM((MEMBERS, CHANNELS, PART), BF16),
            pltpu.VMEM((MEMBERS, CHANNELS, PART), BF16),
            pltpu.VMEM((BLOCKS, 2, 4, 4, 4) + tile, BF16),
            pltpu.VMEM((BLOCKS, 4, 4, 4) + tile, BF16),
            pltpu.VMEM((BLOCKS, 4, 4, 4) + tile, BF16),
            pltpu.VMEM((BLOCKS, 3, 4, 4) + tile, BF16),
            pltpu.VMEM((BLOCKS, 4, 4) + tile, BF16),
            pltpu.VMEM((BLOCKS, 3, 4) + tile, BF16),
            pltpu.VMEM((BLOCKS, 4) + tile, BF16),
            pltpu.VMEM((BLOCKS, 3) + tile, BF16),
            pltpu.VMEM((16, 128), F32),
            pltpu.VMEM((5, 8, 128), F32),
            pltpu.VMEM((10, 8, 128), F32),
            dma((5,)),
            dma((MEMBERS,)),
            dma((MEMBERS,)),
            dma((2, MEMBERS - 1)),
            dma((2, MEMBERS - 1)),
            dma((2, BLOCKS, 10)),
            dma((2, 10)),
        ],
        compiler_params=pltpu.CompilerParams(
            collective_id=0, has_side_effects=True, vmem_limit_bytes=60 * 2**20
        ),
        cost_estimate=pl.CostEstimate(
            flops=2 * LOCAL * HID * (2 * HID + CHANNELS), bytes_accessed=24 * 2**20, transcendentals=LOCAL * HID
        ),
    )(fields, target, area_weights[None, :], hidden, w_in, w_out)
    rows = 1024
    grad_hidden = pl.pallas_call(
        backward_kernel,
        out_shape=jax.ShapeDtypeStruct((1, LOCAL, HID), BF16),
        grid=(LOCAL // rows,),
        in_specs=[
            pl.BlockSpec((rows, HID), lambda i: (i, 0)),
            pl.BlockSpec((HID, HID), lambda i: (0, 0)),
        ],
        out_specs=pl.BlockSpec((1, rows, HID), lambda i: (0, i, 0)),
        compiler_params=pltpu.CompilerParams(vmem_limit_bytes=32 * 2**20),
    )(du, w_in)
    return (loss[0, 0], grad_hidden, grad_w1)


def solution(mesh):
    return jax.shard_map(
        on_device,
        mesh=mesh,
        in_specs=(
            P("member", None, "space"),
            P(None, "space"),
            P("space"),
            P("member", "space", None),
            P(),
            P(),
        ),
        out_specs=(P(), P("member", "space", None), P(("member", "space"), None)),
        check_vma=False,
    )
```

time: 805 us -> 87.9 us (0.11)
  waiting for transfers between devices: 642 us -> 0 us
  Pallas kernels: 0 us -> 81.3 us
  blocking collectives: 65 us -> 0 us
  matrix products: 58.3 us -> 0 us
  other arithmetic: 16.6 us -> 0 us
  between operations: 15.9 us -> 2.43 us
    unnamed x3 -> x0, waiting for transfers between devices: 560 us -> none
    all_gather x1 -> x0, waiting for transfers between devices: 81.5 us -> none  [on_device(): lax.all_gather(fields, 'member', axis=0, tiled=True).astype(jnp.float32)]
    pallas_call x0 -> x2, Pallas kernels: none -> 81.3 us  [the longest x1 70.5 us: on_device(): pl.pallas_call(forward_kernel, out_shape=(jax.ShapeDtypeStruct((1, 1), F3...]
    psum x1 -> x0, blocking collectives: 65 us -> none  [on_device(): lax.psum(local_loss, ('member', 'space')) / (fields.shape[1] * npoints)]
    dot_general x4 -> x0, matrix products: 58.3 us -> none  [the longest x1 16.5 us: on_device(): lax.dot_general(slope, w_out, (((0,), (0,)), ((), ())), preferred_element...]
    reduce_sum x2 -> x0, other arithmetic: 13.4 us -> none  [the longest x1 10.6 us: on_device(): signs = jnp.sum(jnp.sign(gap), 0)]
  transfers between devices with their start and end apart: 2 -> 0, of which waited for: 2 -> 0; matrix products, arithmetic and copies ran while one was open for 4% -> 0% of each run, Pallas kernels for 0% -> 0%
where the time goes in v1:
time: 87.9 us; the launch traced here: 87.7 us
  Pallas kernels  81.3 us (92%)
  local copies, waits for them, and re-layouts  4 us (5%)
  between operations  2.43 us (3%)
    pallas_call x1, Pallas kernels, on_device(): pl.pallas_call(forward_kernel, out_shape=(jax.ShapeDtypeStruct((1, 1), F3...  70.5 us
    pallas_call x1, Pallas kernels, on_device(): pl.pallas_call(backward_kernel, out_shape=jax.ShapeDtypeStruct((1, LOCAL,...  10.8 us
    unnamed x7, local copies, waits for them, and re-layouts  4 us

profile of v1, /device:TPU:0, one launch (start us, length us, event | category | flops | bytes accessed | tf_op | source)
XLA Modules:
  0.0 87.7 jit_solution(13327891008965265267)
XLA Ops:
  0.6 0.0 copy-start.1
  0.6 70.5 %shard_map.85 = (f32[1,1]{1,0:T(1,128)}, bf16[4096,1024]{1,0:T(8,128)(2,1)}, f32[8,1024]{1,0:T(8,128)}) custom-call(bf16[1,100,4096]{2,1,0:T(8,128)(2,1)} %fields.1, bf16[100,4096]{1,0:T(8,128)(2,1)} %target.1, f32[1,4096]{1,0:T(1,128)} %bitcast.2, bf16[1,4096,1024]{2,1,0:T(8,128)(2,1)} %hidden.1, bf16[1024,1024]{1,0:T(8,128)(2,1)} %w_in.3, ...), custom_call_target="tpu_custom_call" | custom-call | flops 18018729984 | bytes 25165824 | tf_op jit(solution)/shard_map/pallas_call | solution.py:358
  71.1 0.0 copy-done.1
  71.1 0.0 copy-start
  71.1 3.4 %copy-done = bf16[4096,1024]{1,0:T(8,128)(2,1)S(1)} copy-done((bf16[4096,1024]{1,0:T(8,128)(2,1)S(1)}, bf16[4096,1024]{1,0:T(8,128)(2,1)}, u32[]{:S(2)}) %copy-start) | copy-done | bytes 8388632
  74.5 0.0 copy-start.2
  74.5 10.8 %shard_map.86 = bf16[1,4096,1024]{2,1,0:T(8,128)(2,1)} custom-call(bf16[4096,1024]{1,0:T(8,128)(2,1)S(1)} %copy-done, bf16[1024,1024]{1,0:T(8,128)(2,1)S(1)} %copy-done.1), custom_call_target="tpu_custom_call" | custom-call | tf_op jit(solution)/shard_map/pallas_call | solution.py:405
  85.9 0.0 copy-done.2
  85.9 0.6 copy.12
Async XLA Ops:
  0.6 70.5 %copy-start.1 = (bf16[1024,1024]{1,0:T(8,128)(2,1)S(1)}, bf16[1024,1024]{1,0:T(8,128)(2,1)}, u32[]{:S(2)}) copy-start(bf16[1024,1024]{1,0:T(8,128)(2,1)} %w_in.3) | copy-start | bytes 6291460
  71.1 3.4 %copy-start = (bf16[4096,1024]{1,0:T(8,128)(2,1)S(1)}, bf16[4096,1024]{1,0:T(8,128)(2,1)}, u32[]{:S(2)}) copy-start(bf16[4096,1024]{1,0:T(8,128)(2,1)} %get-tuple-element.7.du) | copy-start | bytes 25165828
  74.5 11.4 %copy-start.2 = (f32[8,1024]{1,0:T(8,128)S(1)}, f32[8,1024]{1,0:T(8,128)}, u32[]{:S(2)}) copy-start(f32[8,1024]{1,0:T(8,128)} %get-tuple-element.14) | copy-start | bytes 98308
